TPU v7x, 512 devices: a whole 4x8x8 slice. The times are simulated.
512 devices in a mesh: exc: 16 (over z_lo, y), unk: 32 (over z_hi, x, core).
Axes of the slice: x: 4, y: 8, z: 8 (z_hi: 4, z_lo: 2; z = z_hi * 2 + z_lo), core: 2. Of those that a mesh axis runs over, the one named last changes fastest.
Arguments:
- responses: bfloat16 [2, 4, 1440, 16384], P(None, None, 'exc', 'unk'), may hold values from -6 to 6
- eigvecs: bfloat16 [1440, 11520], P('exc'), may hold values from -0.15625 to 0.15625
Outputs:
- gram: float32 [2, 4, 1440, 1440], P(None, None, 'exc', 'unk')
- basis: bfloat16 [2, 4, 1440, 16384], P(None, None, 'exc', 'unk')
All inputs are finite; a program needn't handle non-finite values.
Results may differ from a plain program's by a relative error of at most 0.0005.
Values may be sent and summed in bfloat16 or wider, within the bound.
A program may use at most 128 MiB of HBM per device.

v0:
```python
import jax
import jax.numpy as jnp
from jax import lax
from jax.sharding import PartitionSpec as P


def gram_tile(local_part, other_part, unknowns):
    prods = jnp.einsum(
        "pbgr,qblr->pqbgl", local_part, other_part, preferred_element_type=jnp.float32
    )
    return jnp.stack([prods[0, 0] + prods[1, 1], prods[0, 1] - prods[1, 0]]) / unknowns


def basis_terms(part_rows, eig_rows):
    prods = jnp.einsum("kqbl,pblr->pqbkr", eig_rows, part_rows, preferred_element_type=jnp.float32)
    return jnp.stack([prods[0, 0] - prods[1, 1], prods[1, 0] + prods[0, 1]])


def local(responses, eigvecs):
    groups = lax.axis_size("exc")
    block_count = responses.shape[1]
    group_width = responses.shape[2]
    row_count = responses.shape[3]
    total_waves = group_width * groups
    kept_rows = eigvecs.shape[0]
    eigen_division = eigvecs.reshape(kept_rows, 2, block_count, total_waves)
    unknowns = float(row_count * lax.axis_size("unk"))
    shard_piece = lax.all_gather(responses, "exc", axis=2, tiled=True)
    tile_cols = gram_tile(responses, shard_piece, unknowns)
    gram_row = tile_cols
    gram_row, basis_sum = (gram_row, basis_terms(shard_piece, eigen_division))
    gram_portion = lax.psum_scatter(gram_row, "unk", scatter_dimension=3, tiled=True)
    return (gram_portion, basis_sum.astype(jnp.bfloat16))


def solution(mesh):
    in_specs = (P(None, None, "exc", "unk"), P("exc", None))
    out_specs = (P(None, None, "exc", "unk"), P(None, None, "exc", "unk"))
    return jax.shard_map(local, mesh=mesh, in_specs=in_specs, out_specs=out_specs, check_vma=False)
```

profile of v0, /device:TPU:1, one launch (start us, length us, event | category | flops | bytes accessed | tf_op | source)
XLA Modules:
  0.0 507.9 jit_solution(291565054956885942)
XLA Ops:
  7.2 0.0 all-gather.2.cloned.1.call-start
  7.2 2.2 copy.13
  9.4 0.0 all-gather.2.cloned.1.call-update
  9.5 0.0 all-reduce.3.cloned.1.call-start
  9.5 144.4 %all-gather.2.cloned.1.call-done = bf16[2,4,1440,512]{3,1,0,2:T(4,128)(2,1)} async-done(((bf16[2,4,90,512]{3,1,0,2:T(4,128)(2,1)}), bf16[2,4,1440,512]{3,1,0,2:T(4,128)(2,1)}) %all-gather.2.cloned.1.call-update) | async-done | bytes 11796496 | tf_op jit(solution)/shard_map/all_gather | solution.py:28
  153.9 15.4 %fusion.4 = f32[2,2,4,90,1440]{4,3,0,1,2:T(8,128)} fusion(bf16[2,4,1440,512,1]{3,1,0,2,4:T(4,128)(2,1)} %bitcast.41, bf16[2,4,90,512,1]{3,1,2,0,4:T(4,128)(2,1)} %bitcast.43), kind=kOutput, calls=%fused_computation.4 | convolution fusion | flops 2123366400 | bytes 20828160 | tf_op jit(solution)/shard_map/pbgr,qblr->pqbgl/dot_general | solution.py:8
  169.3 2.8 fusion.7
  172.0 2.8 fusion.9
  174.8 2.9 maximum_multiply_fusion
  177.7 7.0 %copy.18 = f32[2,4,90,1440]{2,1,0,3:T(4,128)} copy(f32[2,4,90,1440]{3,2,1,0:T(8,128)} %maximum_multiply_fusion) | data formatting | bytes 8294400 | tf_op jit(solution)/shard_map/div | solution.py:11
  184.7 0.0 copy-start
  184.7 0.0 all-reduce.3.cloned.1.call-update
  184.7 1.6 copy-done
  186.3 5.1 reshape.81
  191.4 1.3 dynamic-slice
  193.3 12.6 %fusion.11 = f32[2,2,4,90,512]{4,3,1,0,2:T(8,128)S(1)} fusion(bf16[90,2,4,1440,1]{3,2,1,0,4:T(4,128)(2,1)} %bitcast.44, bf16[2,4,1440,512,1]{3,1,0,2,4:T(4,128)(2,1)} %bitcast.42), kind=kOutput, calls=%fused_computation.13 | convolution fusion | flops 2123366400 | bytes 16819200 | tf_op jit(solution)/shard_map/kqbl,pblr->pqbkr/dot_general | solution.py:15
  205.9 0.1 fusion.21
  206.0 0.1 fusion.20
  206.1 0.1 pad_maximum_fusion
  206.2 1.4 copy.24
  207.6 291.8 %all-reduce.3.cloned.1.call-done = f32[2,4,90,1440]{2,1,0,3:T(4,128)} async-done(((f32[2,4,90,1440]{2,1,0,3:T(4,128)}), f32[2,4,90,1440]{2,1,0,3:T(4,128)}) %all-reduce.3.cloned.1.call-update) | async-done | bytes 4147216
  499.4 0.9 constant_dynamic-slice_fusion
  500.4 0.7 copy.23
Async XLA Ops:
  7.2 146.7 %all-gather.2.cloned.1.call-start = ((), (), s32[]{:S(2)}) async-start(), calls=%async_computation | async-start | bytes 12533760 | tf_op jit(solution)/shard_map/all_gather | solution.py:28
  9.5 490.0 %all-reduce.3.cloned.1.call-start = ((), (), s32[]{:S(2)}) async-start(), calls=%async_computation.1 | async-start | bytes 11796480
  184.7 1.6 copy-start
Sparse Core Ops, SparseCore 0:
  10.7 143.1 all-gather.1
  184.8 314.5 all-reduce.2
where the time goes:
time: 509 us; the launch traced here: 508 us
  waiting for transfers between devices  436 us (86%)
  matrix products  28 us (6%)
  local copies, waits for them, and re-layouts  20.2 us (4%)
  between operations  14.7 us (3%)
  other arithmetic  8.68 us (2%)
    unnamed x3, waiting for transfers between devices  292 us
    all_gather x1, waiting for transfers between devices, local(): shard_piece = lax.all_gather(responses, 'exc', axis=2, tiled=True)  144 us
    dot_general x1, matrix products, gram_tile(): jnp.einsum('pbgr,qblr->pqbgl', local_part, other_part, preferred_element_...  15.4 us
    dot_general x1, matrix products, basis_terms(): jnp.einsum('kqbl,pblr->pqbkr', eig_rows, part_rows, preferred_element_typ...  12.6 us
  transfers between devices with their start and end apart: 2, of which 2 were waited for; matrix products, arithmetic and copies ran while one was open for 4% of the time, Pallas kernels for 0%

commit v1 on v0

v1 whole, which is shorter than its diff:
```python
import jax
import jax.numpy as jnp
from jax import lax
from jax.experimental import pallas as pl
from jax.experimental.pallas import tpu as pltpu
from jax.sharding import PartitionSpec as P

MESH = pl.DeviceIdType.MESH
ROWS, PAD, HALF = 90, 96, 256
BLOCKS, RING, GROUPS = 4, 8, 16
WAVES = ROWS * GROUPS
KDIM = PAD * GROUPS
F32 = jnp.float32


def mod(value, size):
    return lax.rem(value + 2 * size, size)


def device(x, y, zh, zl, c):
    return {"exc": zl * 8 + y, "unk": (zh * 4 + x) * 2 + c}


def pick(flag, one, other):
    return flag * one + (1 - flag) * other


def kernel(
    x_ref, e_ref, basis_ref, gram_ref,
    xs, staged, ee, bsend, bland, parts, core_in, x1_in, x2_in, zl_in, zh_in, zsum, done, fin_in,
    pair_s, pair_r, ring_s, ring_r, eig_s, eig_r, fwd_s, fwd_r, out_s, out_r,
    core_s, core_r, x1_s, x1_r, x2_s, x2_r, zl_s, zl_r, zh_s, zh_r, fin_s, fin_r,
):
    exc, unk = lax.axis_index("exc"), lax.axis_index("unk")
    zl, y = exc // 8, exc % 8
    zh, x, c = unk // 8, (unk // 2) % 4, unk % 2
    other = 1 - zl
    up, down = device(x, mod(y + 1, 8), zh, zl, c), device(x, mod(y - 1, 8), zh, zl, c)
    pair = device(x, y, zh, other, c)
    znext = device(x, y, mod(zh + zl, 4), other, c)
    zprev = device(x, y, mod(zh - other, 4), other, c)
    sibling = device(x, y, zh, zl, 1 - c)
    xup, xdown = device(mod(x + 1, 4), y, zh, zl, c), device(mod(x - 1, 4), y, zh, zl, c)
    zothers = [device(x, y, mod(zh + k, 4), zl, c) for k in (1, 2, 3)]
    kap = mod(x - y, 4)
    jy = mod(y + kap - 4 * (kap // 3), 8)
    plus = jnp.where((kap == 0) | (kap == 3), 1, 0)
    ioff = pick(plus, kap // 3 + c, -(kap // 2 + c))
    iy = mod(y + ioff, 8)
    dest_zh = zl * 2 + jy // 4
    dests = [(zi, cc) for zi in (0, 1) for cc in (0, 1)]
    is_self = [(iy == y) & (dest_zh == zh) & (zl == zi) & (c == cc) for zi, cc in dests]
    my_j = (zh % 2) * 4 + x
    delta = mod(my_j - y, 8)
    src_y = jnp.where(
        delta == 0, my_j,
        jnp.where(delta == 7, my_j,
        jnp.where(delta <= 2, mod(my_j - 1, 8),
        jnp.where(delta <= 4, mod(my_j - 2, 8), mod(my_j + 1, 8)))))
    src_c = jnp.where((delta == 7) | (delta == 2) | (delta == 4) | (delta == 5), 1, 0)
    src_zl = zh // 2
    from_self = [(src_y == y) & (src_zl == zl) & (src_c == c) & (zh == g) for g in range(4)]

    def remote(src, dst, send, recv, to):
        return pltpu.make_async_remote_copy(
            src_ref=src, dst_ref=dst, send_sem=send, recv_sem=recv, device_id=to, device_id_type=MESH
        )

    barrier = pltpu.get_barrier_semaphore()

    def greet(to):
        pl.semaphore_signal(barrier, inc=1, device_id=to, device_id_type=MESH)

    around = [up, down, znext, zprev, sibling, xup, xdown] + zothers
    for to in around:
        greet(to)
    for g in range(4):
        pl.when(jnp.logical_not(from_self[g]))(lambda g=g: greet(device(x, src_y, g, src_zl, src_c)))
    selves = sum(jnp.where(f, 1, 0) for f in is_self)
    pl.semaphore_wait(barrier, len(around) + 4 - selves)

    zero = jnp.zeros((16, 2 * HALF), jnp.bfloat16)

    def pair_copy(b):
        return remote(staged.at[b], xs.at[b, zl, y], pair_s.at[b], pair_r.at[b], pair)

    def pair_recv(b):
        return remote(staged.at[b], xs.at[b, other, y], pair_s.at[b], pair_r.at[b], pair)

    for b in range(BLOCKS):
        p, q = x_ref[0, b], x_ref[1, b]
        low = jnp.concatenate([p[:, :HALF], q[:, :HALF]], axis=1)
        high = jnp.concatenate([p[:, HALF:], q[:, HALF:]], axis=1)
        first = jnp.full(low.shape, zl, jnp.int32) == 0
        staged[b, 80:96, :] = zero
        staged[b, 0:ROWS, :] = jnp.where(first, high, low)
        pair_copy(b).start()
        xs[b, zl, y, 80:96, :] = zero
        xs[b, zl, y, 0:ROWS, :] = jnp.where(first, low, high)

    def ring(way, b, d):
        src = mod(y - (d - 1), 8) if way == 0 else mod(y + (d - 1), 8)
        ref = xs.at[b, :, src] if d < 4 else xs.at[b, way, src]
        return remote(ref, ref, ring_s.at[way, b, d - 1], ring_r.at[way, b, d - 1], (up, down)[way])

    def ring_recv(way, b, d):
        src = mod(y - d, 8) if way == 0 else mod(y + d, 8)
        ref = xs.at[b, :, src] if d < 4 else xs.at[b, way, src]
        return remote(ref, ref, ring_s.at[way, b, d - 1], ring_r.at[way, b, d - 1], (up, down)[way])

    def pack_eig(b):
        for part in range(2):
            ee[b, 0, part] = jnp.zeros((PAD, KDIM), jnp.bfloat16)
            base = (part * BLOCKS + b) * WAVES
            for i in range(GROUPS):
                ee[b, 0, part, 0:ROWS, i * PAD : i * PAD + ROWS] = e_ref[:, base + i * ROWS : base + (i + 1) * ROWS]

    def eig_copy(k):
        b = 2 * k + c
        return remote(ee.at[b, 0], ee.at[b, 1], eig_s.at[k], eig_r.at[k], (znext, zprev)[k])

    def eig_recv(k):
        b = 2 * k + c
        return remote(ee.at[b, 0], ee.at[b, 1], eig_s.at[k], eig_r.at[k], (znext, zprev)[k])

    def eig_forward(k):
        b = 2 * k + c
        return remote(ee.at[b, 1], ee.at[b, 1], fwd_s.at[k], fwd_r.at[k], sibling)

    def eig_forward_recv(k):
        b = 2 * k + 1 - c
        return remote(ee.at[b, 1], ee.at[b, 1], fwd_s.at[k], fwd_r.at[k], sibling)

    def gram_partial(b):
        def one(t, _):
            k, s = t // 2, t % 2
            joff = k - 4 * (k // 3)
            pos = jnp.where((k == 0) | (k == 3), 1, 0)
            off = pick(pos, k // 3 + s, -(k // 2 + s))
            rows = xs[b, :, mod(y + joff, 8)].reshape(2 * PAD, 2 * HALF)
            cols = []
            for zi in range(2):
                v = xs[b, zi, mod(y + off, 8)]
                cols += [v, jnp.concatenate([-v[:, HALF:], v[:, :HALF]], axis=1)]
            right = jnp.concatenate(cols, axis=0)
            parts[b, s, k] = lax.dot_general(rows, right, (((1,), (1,)), ((), ())), preferred_element_type=F32)
            return 0

        lax.fori_loop(0, 8, one, 0)
        core_copy(b).start()

    def core_copy(b):
        return remote(parts.at[b, 1 - c], core_in.at[b], core_s.at[b], core_r.at[b], sibling)

    k_up, k_down, k_far = mod(x + 1 - y, 4), mod(x - 1 - y, 4), mod(x + 2 - y, 4)

    def x1_copy(b, way):
        return remote(
            parts.at[b, c, k_far, way * PAD : (way + 1) * PAD], x1_in.at[b, way],
            x1_s.at[b, way], x1_r.at[b, way], (xup, xdown)[way],
        )

    def x2_copy(b, way):
        return remote(
            parts.at[b, c, (k_up, k_down)[way]], x2_in.at[b, way], x2_s.at[b, way], x2_r.at[b, way], (xup, xdown)[way]
        )

    def zl_copy(b):
        rows = pl.ds(pl.multiple_of(other * PAD, PAD), PAD)
        return remote(parts.at[b, c, kap, rows], zl_in.at[b], zl_s.at[b], zl_r.at[b], pair)

    def zh_copy(b, k):
        rows = pl.ds(pl.multiple_of(mod(zh + k, 4) * 24, 8), 24)
        return remote(zsum.at[b, rows], zh_in.at[b, k - 1], zh_s.at[b, k - 1], zh_r.at[b, k - 1], zothers[k - 1])

    def stage_core(b):
        core_copy(b).wait_recv()

        def add(k, _):
            parts[b, c, k] += core_in[b, k]
            return 0

        lax.fori_loop(0, 4, add, 0)
        x1_copy(b, 0).start()
        x1_copy(b, 1).start()

    def stage_x1(b):
        for way, k in ((0, k_up), (1, k_down)):
            x1_copy(b, way).wait_recv()
            parts[b, c, k, way * PAD : (way + 1) * PAD] += x1_in[b, way]
            x2_copy(b, way).start()

    def stage_x2(b):
        x2_copy(b, 0).wait_recv()
        x2_copy(b, 1).wait_recv()
        parts[b, c, kap] += x2_in[b, 0] + x2_in[b, 1]
        zl_copy(b).start()

    def stage_zl(b):
        zl_copy(b).wait_recv()
        rows = pl.ds(pl.multiple_of(zl * PAD, PAD), PAD)
        zsum[b] = parts[b, c, kap, rows] + zl_in[b]
        for k in (1, 2, 3):
            zh_copy(b, k).start()

    def fin_rows(g):
        return pl.ds(pl.multiple_of(g * 24, 8), 24)

    def fin_copy(b, n):
        zi, cc = dests[n]
        return remote(
            done.at[b, :, zi * 128 : zi * 128 + 256], fin_in.at[b, fin_rows(zh)],
            fin_s.at[b, n], fin_r.at[b, zh], device(x, iy, dest_zh, zi, cc),
        )

    def fin_local(b, n):
        zi, cc = dests[n]
        return pltpu.make_async_copy(
            done.at[b, :, zi * 128 : zi * 128 + 256], fin_in.at[b, fin_rows(zh)], fin_r.at[b, zh]
        )

    def stage_zh(b):
        for k in (1, 2, 3):
            zh_copy(b, k).wait_recv()
        done[b] = zsum[b, fin_rows(zh)] + zh_in[b, 0] + zh_in[b, 1] + zh_in[b, 2]
        for n in range(4):
            pl.when(is_self[n])(lambda n=n: fin_local(b, n).start())
            pl.when(jnp.logical_not(is_self[n]))(lambda n=n: fin_copy(b, n).start())

    def stage_fin(b):
        for g in range(4):
            remote(
                done.at[b, :, 0:256], fin_in.at[b, fin_rows(g)], fin_s.at[b, 0], fin_r.at[b, g], sibling
            ).wait_recv()
        gram_ref[b] = fin_in[b] * (1.0 / 16384.0)

    def out_copy(b):
        return remote(bsend.at[b], bland.at[b], out_s.at[b], out_r.at[b], pair)

    mine = pl.ds(pl.multiple_of(zl * HALF, HALF), HALF)
    theirs = pl.ds(pl.multiple_of(other * HALF, HALF), HALF)

    def basis(b):
        waves = xs[b].reshape(KDIM, 2 * HALF)
        for slot in (1, 0):
            rows = ee[b, slot].reshape(2 * PAD, KDIM)
            prod = jnp.dot(rows, waves, preferred_element_type=F32)
            re = (prod[:PAD, :HALF] - prod[PAD:, HALF:]).astype(jnp.bfloat16)
            im = (prod[PAD:, :HALF] + prod[:PAD, HALF:]).astype(jnp.bfloat16)
            if slot == 1:
                bsend[b, 0] = re
                bsend[b, 1] = im
                out_copy(b).start()
            else:
                basis_ref[0, b, :, mine] = re
                basis_ref[1, b, :, mine] = im

    def basis_land(b):
        out_copy(b).wait_recv()
        for part in range(2):
            basis_ref[part, b, :, theirs] = bland[b, part]

    for b in (0, 1, 2, 3):
        pair_recv(b).wait_recv()
        for way in (0, 1):
            ring(way, b, 1).start()
    pack_eig(0)
    pack_eig(1)

    def eig_a():
        eig_copy(0).start()

    def eig_b():
        pack_eig(2)

    def eig_c():
        pack_eig(3)
        eig_copy(1).start()

    def eig_d(k):
        eig_recv(k).wait_recv()
        eig_forward(k).start()

    todo = {
        0: [eig_a, eig_b],
        1: [eig_c],
        2: [lambda: gram_partial(0)],
        3: [lambda: stage_core(0), lambda: gram_partial(1)],
        4: [lambda: stage_core(1)],
        5: [lambda: stage_x1(0)],
        6: [lambda: stage_x1(1), lambda: gram_partial(2)],
        7: [lambda: stage_core(2), lambda: gram_partial(3)],
        8: [lambda: stage_x2(0), lambda: stage_core(3), lambda: eig_d(0)],
        9: [lambda: stage_x1(2), lambda: stage_zl(0), lambda: stage_x2(1)],
        10: [lambda: stage_x1(3), lambda: stage_zl(1), lambda: stage_zh(0), lambda: eig_d(1)],
        11: [lambda: stage_x2(2), lambda: stage_zh(1)],
        12: [lambda: stage_fin(0), lambda: stage_zl(2), lambda: stage_x2(3)],
        13: [lambda: stage_fin(1), lambda: stage_zl(3)],
        14: [lambda: stage_zh(2)],
        15: [lambda: stage_zh(3)],
    }
    order = [(0, 1), (1, 1), (0, 2), (1, 2), (2, 1), (3, 1), (2, 2), (3, 2)]
    order += [(b, d) for d in (3, 4) for b in range(BLOCKS)]
    for slot, (b, d) in enumerate(order):
        for way in (0, 1):
            ring_recv(way, b, d).wait_recv()
            if d < 4:
                ring(way, b, d + 1).start()
        if slot == 12:
            eig_forward_recv(0).wait_recv()
            eig_forward_recv(1).wait_recv()
        if d == 4:
            basis(b)
        for act in todo.get(slot, ()):
            act()
    stage_fin(2)
    stage_fin(3)
    for b in range(BLOCKS):
        basis_land(b)

    for b in range(BLOCKS):
        pair_copy(b).wait_send()
        for d in (1, 2, 3, 4):
            for way in (0, 1):
                ring(way, b, d).wait_send()
        out_copy(b).wait_send()
        core_copy(b).wait_send()
        for way in (0, 1):
            x1_copy(b, way).wait_send()
            x2_copy(b, way).wait_send()
        zl_copy(b).wait_send()
        for k in (1, 2, 3):
            zh_copy(b, k).wait_send()
        for n in range(4):
            pl.when(jnp.logical_not(is_self[n]))(lambda n=n, b=b: fin_copy(b, n).wait_send())
    for k in (0, 1):
        eig_copy(k).wait_send()
        eig_forward(k).wait_send()


def local(responses, eigvecs):
    dma = pltpu.SemaphoreType.DMA
    bf, vm = jnp.bfloat16, pltpu.VMEM
    basis, gram = pl.pallas_call(
        kernel,
        out_shape=(
            jax.ShapeDtypeStruct((2, BLOCKS, PAD, 2 * HALF), bf),
            jax.ShapeDtypeStruct((BLOCKS, PAD, 256), F32),
        ),
        in_specs=[pl.BlockSpec(memory_space=vm)] * 2,
        out_specs=(pl.BlockSpec(memory_space=vm),) * 2,
        scratch_shapes=[
            vm((BLOCKS, 2, RING, PAD, 2 * HALF), bf),
            vm((BLOCKS, PAD, 2 * HALF), bf),
            vm((BLOCKS, 2, 2, PAD, KDIM), bf),
            vm((BLOCKS, 2, PAD, HALF), bf),
            vm((BLOCKS, 2, PAD, HALF), bf),
            vm((BLOCKS, 2, 4, 2 * PAD, 4 * PAD), F32),
            vm((BLOCKS, 4, 2 * PAD, 4 * PAD), F32),
            vm((BLOCKS, 2, PAD, 4 * PAD), F32),
            vm((BLOCKS, 2, 2 * PAD, 4 * PAD), F32),
            vm((BLOCKS, PAD, 4 * PAD), F32),
            vm((BLOCKS, 3, 24, 4 * PAD), F32),
            vm((BLOCKS, PAD, 4 * PAD), F32),
            vm((BLOCKS, 24, 4 * PAD), F32),
            vm((BLOCKS, PAD, 256), F32),
            dma((4,)), dma((4,)), dma((2, 4, 4)), dma((2, 4, 4)),
            dma((2,)), dma((2,)), dma((2,)), dma((2,)), dma((4,)), dma((4,)),
            dma((4,)), dma((4,)), dma((4, 2)), dma((4, 2)), dma((4, 2)), dma((4, 2)),
            dma((4,)), dma((4,)), dma((4, 3)), dma((4, 3)), dma((4, 4)), dma((4, 4)),
        ],
        compiler_params=pltpu.CompilerParams(
            collective_id=0, has_side_effects=True, vmem_limit_bytes=60 * 2**20
        ),
    )(responses, eigvecs)
    zl = lax.axis_index("exc") // 8
    c = lax.axis_index("unk") % 2
    mine = lax.dynamic_slice(gram, (0, c * 45, zl * 64), (BLOCKS, 45, 2 * PAD))
    mine = mine.reshape(BLOCKS, 45, 2, PAD)[..., :ROWS]
    return jnp.transpose(mine, (2, 0, 3, 1)), basis[:, :, :ROWS]


def solution(mesh):
    specs = P(None, None, "exc", "unk")
    return jax.shard_map(local, mesh=mesh, in_specs=(specs, P("exc", None)), out_specs=(specs, specs), check_vma=False)
```

time: 509 us -> 133 us (0.26)
  waiting for transfers between devices: 436 us -> 0 us
  Pallas kernels: 0 us -> 126 us
  matrix products: 28 us -> 0 us
  between operations: 14.7 us -> 0.69 us
  local copies, waits for them, and re-layouts: 20.2 us -> 6.67 us
  other arithmetic: 8.68 us -> 0 us
    unnamed x3 -> x0, waiting for transfers between devices: 292 us -> none
    all_gather x1 -> x0, waiting for transfers between devices: 144 us -> none  [local(): shard_piece = lax.all_gather(responses, 'exc', axis=2, tiled=True)]
    pallas_call x0 -> x1, Pallas kernels: none -> 126 us  [local(): pl.pallas_call(kernel, out_shape=(jax.ShapeDtypeStruct((2, BLOCKS, PAD, 2...]
    dot_general x2 -> x0, matrix products: 28 us -> none  [the longest x1 15.4 us: gram_tile(): jnp.einsum('pbgr,qblr->pqbgl', local_part, other_part, preferred_element_...]
    div x1 -> x0, local copies, waits for them, and re-layouts: 6.99 us -> none  [gram_tile(): jnp.stack([prods[0, 0] + prods[1, 1], prods[0, 1] - prods[1, 0]]) / unknowns]
  transfers between devices with their start and end apart: 2 -> 0, of which waited for: 2 -> 0; matrix products, arithmetic and copies ran while one was open for 4% -> 0% of each run, Pallas kernels for 0% -> 0%
where the time goes in v1:
time: 133 us
  Pallas kernels  126 us (95%)
  local copies, waits for them, and re-layouts  6.67 us (5%)
    pallas_call x1, Pallas kernels, local(): pl.pallas_call(kernel, out_shape=(jax.ShapeDtypeStruct((2, BLOCKS, PAD, 2...  126 us
    unnamed x3, local copies, waits for them, and re-layouts  5.43 us

profile of v1, /device:TPU:1, one launch (start us, length us, event | category | flops | bytes accessed | tf_op | source)
XLA Modules:
  0.0 133.0 jit_solution(15101782460343590579)
XLA Ops:
  0.6 2.1 %copy.6.x_ref = bf16[2,4,90,512]{3,2,1,0:T(8,128)(2,1)} copy(bf16[2,4,90,512]{3,1,2,0:T(4,128)(2,1)} %param.2) | data formatting | bytes 1474560 | tf_op args[0]
  2.8 125.6 %shard_map.41 = (bf16[2,4,96,512]{3,2,1,0:T(8,128)(2,1)}, f32[4,96,256]{2,1,0:T(8,128)}) custom-call(bf16[2,4,90,512]{3,2,1,0:T(8,128)(2,1)} %copy.6.x_ref, bf16[90,11520]{1,0:T(8,128)(2,1)} %e_ref.1), custom_call_target="tpu_custom_call" | custom-call | tf_op jit(solution)/shard_map/pallas_call | solution.py:344
  128.4 1.1 constant_dynamic-slice_fusion
  129.5 0.2 reshape.8
  129.7 0.7 copy.8
  130.4 2.6 %copy.9 = bf16[2,4,90,512]{3,1,2,0:T(4,128)(2,1)} copy(bf16[2,4,90,512]{3,2,1,0:T(8,128)(2,1)} %bitcast.4) | data formatting | bytes 1474560
  (1 shorter events, 0.0 us)

commit v2 on v0

v2 whole, which is shorter than its diff:
```python
import jax
import jax.numpy as jnp
from jax import lax
from jax.experimental import pallas as pl
from jax.experimental.pallas import tpu as pltpu
from jax.sharding import PartitionSpec as P

MESH = pl.DeviceIdType.MESH
ROWS, PAD, HALF = 90, 96, 256
BLOCKS, RING, GROUPS = 4, 8, 16
WAVES = ROWS * GROUPS
KDIM = PAD * GROUPS
ZH_SLOT = 1
CUT = 56
F32 = jnp.float32


def mod(value, size):
    return lax.rem(value + 2 * size, size)


def device(x, y, zh, zl, c):
    return {"exc": zl * 8 + y, "unk": (zh * 4 + x) * 2 + c}


def row_of(k):
    return k - 4 * (k // 3)


def col_of(k, s):
    plus = jnp.where((k == 0) | (k == 3), 1, 0)
    return plus * (k // 3 + s) - (1 - plus) * (k // 2 + s)


def kernel(
    x_ref, e_ref, basis_ref, gram_ref,
    xs, staged, window, ee, bsend, bland, parts, core_in, zl_in, zsum, zh_in, done, fin_in,
    scat_s, scat_r, near_s, near_r, ring_s, ring_r, win_s, eig_s, eig_r, fwd_s, fwd_r, out_s, out_r,
    core_s, core_r, zl_s, zl_r, zh_s, zh_r, fin_s, fin_r, above,
):
    exc, unk = lax.axis_index("exc"), lax.axis_index("unk")
    zl, y = exc // 8, exc % 8
    zh, x, c = unk // 8, (unk // 2) % 4, unk % 2
    other = 1 - zl
    up, down = device(x, mod(y + 1, 8), zh, zl, c), device(x, mod(y - 1, 8), zh, zl, c)
    pair = device(x, y, zh, other, c)
    sibling = device(x, y, zh, zl, 1 - c)
    pool = [(o, t) for o in (0, 1, 3, 2) for t in (0, 1) if (o, t) != (0, 0)]

    def pooled(o, t):
        return device(mod(x + o, 4), y, zh, (zl, other)[t], c)

    jy, iy = mod(y + row_of(zh), 8), mod(y + col_of(zh, c), 8)
    dests = [(zi, cc) for zi in (0, 1) for cc in (0, 1)]
    dest_x, dest_zh = jy % 4, zl * 2 + jy // 4
    same = (dest_x == x) & (iy == y) & (dest_zh == zh)
    is_self = [same & (zl == zi) & (c == cc) for zi, cc in dests]
    def remote(src, dst, send, recv, to):
        return pltpu.make_async_remote_copy(
            src_ref=src, dst_ref=dst, send_sem=send, recv_sem=recv, device_id=to, device_id_type=MESH
        )

    def win_copy(part):
        first = pl.multiple_of((part * 4 + x) * 1408 + part * 128, 128)
        return pltpu.make_async_copy(e_ref.at[:, pl.ds(first, KDIM)], window.at[part], win_s.at[part])

    win_copy(0).start()
    win_copy(1).start()

    barrier = pltpu.get_barrier_semaphore()

    def greet(to):
        pl.semaphore_signal(barrier, inc=1, device_id=to, device_id_type=MESH)

    around = [up, down, sibling] + [pooled(o, t) for o, t in pool]
    for to in around:
        greet(to)
    for k in (1, 2, 3):
        pl.when(zh < k)(lambda k=k: greet(device(x, y, k, zl, c)))
    pl.semaphore_wait(barrier, len(around) + zh)
    for k in (0, 1, 2):

        @pl.when(zh > k)
        def _():
            pl.semaphore_signal(above, inc=1, device_id=device(x, y, k, zl, c), device_id_type=MESH)

    zero = jnp.zeros((PAD - 80, 2 * HALF), jnp.bfloat16)

    def scat_copy(o, t):
        return remote(staged.at[mod(x + o, 4), t], xs.at[x, zl, y], scat_s.at[o, t], scat_r.at[x, zl], pooled(o, t))

    def scat_recv(o, t):
        q, z = mod(x + o, 4), (zl, other)[t]
        return remote(staged.at[q, t], xs.at[q, z, y], scat_s.at[o, t], scat_r.at[q, z], pooled(o, t))

    def near(way, o, t):
        q, z = mod(x + o, 4), (zl, other)[t]
        ref = xs.at[q, z, y]
        return remote(ref, ref, near_s.at[way, o, t], near_r.at[way, q, z], (up, down)[way])

    def near_recv(way, o, z):
        q = mod(x + o, 4)
        ref = xs.at[q, z, mod(y - 1, 8) if way == 0 else mod(y + 1, 8)]
        return remote(ref, ref, near_s.at[way, o, z], near_r.at[way, q, z], (up, down)[way])

    def ring_ref(way, o, d, hop):
        src = mod(y - hop, 8) if way == 0 else mod(y + hop, 8)
        q = mod(x + o, 4)
        return xs.at[q, :, src] if d < 4 else xs.at[q, way, src]

    def ring(way, o, d):
        ref = ring_ref(way, o, d, d - 1)
        return remote(ref, ref, ring_s.at[way, o, d - 2], ring_r.at[way, o, d - 2], (up, down)[way])

    def ring_recv(way, o, d):
        ref = ring_ref(way, o, d, d)
        return remote(ref, ref, ring_s.at[way, o, d - 2], ring_r.at[way, o, d - 2], (up, down)[way])

    for o in (0, 1, 3, 2):
        b = mod(x + o, 4)
        p, q = x_ref[0, b], x_ref[1, b]
        low = jnp.concatenate([p[:, :HALF], q[:, :HALF]], axis=1)
        high = jnp.concatenate([p[:, HALF:], q[:, HALF:]], axis=1)
        first = jnp.full(low.shape, zl, jnp.int32) == 0
        staged[b, 1, 80:96, :] = zero
        staged[b, 1, 0:ROWS, :] = jnp.where(first, high, low)
        scat_copy(o, 1).start()
        if o == 0:
            xs[b, zl, y, 80:96, :] = zero
            xs[b, zl, y, 0:ROWS, :] = jnp.where(first, low, high)
            near(0, 0, 0).start()
            near(1, 0, 0).start()
        else:
            staged[b, 0, 80:96, :] = zero
            staged[b, 0, 0:ROWS, :] = jnp.where(first, low, high)
            scat_copy(o, 0).start()

    def pack_eig():
        win_copy(0).wait()
        win_copy(1).wait()
        for part in range(2):
            ee[0, part] = jnp.zeros((PAD, KDIM), jnp.bfloat16)
        for at in range(4):

            @pl.when(x == at)
            def _():
                for part in range(2):
                    for i in range(GROUPS):
                        first = at * 32 + i * ROWS
                        ee[0, part, 0:ROWS, i * PAD : i * PAD + ROWS] = window[part, :, first : first + ROWS]

    def eig_copy():
        return remote(ee.at[0, c], ee.at[1, c], eig_s, eig_r, pair)

    def eig_forward():
        return remote(ee.at[1, c], ee.at[1, c], fwd_s, fwd_r, sibling)

    def eig_forward_recv():
        return remote(ee.at[1, 1 - c], ee.at[1, 1 - c], fwd_s, fwd_r, sibling)

    def gram_partial(n, o):
        q = mod(x + o, 4)

        def one(t, _):
            k, s = 2 * n + t // 2, t % 2
            rows = xs[q, :, mod(y + row_of(k), 8)].reshape(2 * PAD, 2 * HALF)
            cols = []
            for zi in range(2):
                v = xs[q, zi, mod(y + col_of(k, s), 8)]
                cols += [v, jnp.concatenate([-v[:, HALF:], v[:, :HALF]], axis=1)]
            right = jnp.concatenate(cols, axis=0)
            prod = lax.dot_general(rows, right, (((1,), (1,)), ((), ())), preferred_element_type=F32)
            parts[n, s, t // 2] += prod
            return 0

        lax.fori_loop(0, 4, one, 0)

    def core_copy(n):
        return remote(parts.at[n, 1 - c], core_in.at[n], core_s.at[n], core_r.at[n], sibling)

    def zl_copy(n):
        rows = pl.ds(pl.multiple_of(other * PAD, PAD), PAD)
        return remote(parts.at[n, c, :, rows], zl_in.at[n], zl_s.at[n], zl_r.at[n], pair)

    def zh_copy(k):
        slot = mod(zh - k, 4) - 1
        return remote(zsum.at[k], zh_in.at[slot], zh_s.at[k], zh_r.at[slot], device(x, y, k, zl, c))

    def zh_recv(slot):
        return remote(zsum.at[0], zh_in.at[slot], zh_s.at[0], zh_r.at[slot], sibling)

    def stage_core(n):
        core_copy(n).wait_recv()
        for k in range(2):
            parts[n, c, k] += core_in[n, k]
        zl_copy(n).start()

    def stage_zl(n):
        zl_copy(n).wait_recv()
        rows = pl.ds(pl.multiple_of(zl * PAD, PAD), PAD)
        for k in range(2):
            zsum[2 * n + k] = parts[n, c, k, rows] + zl_in[n, k]
            pl.when(zh != 2 * n + k)(lambda k=k: zh_copy(2 * n + k).start())

    def fin_refs(n):
        zi, cc = dests[n]
        return done.at[40 * cc : 40 * cc + CUT, zi * 128 : zi * 128 + 256], fin_in.at[x]

    def fin_copy(n):
        zi, cc = dests[n]
        src, dst = fin_refs(n)
        return remote(src, dst, fin_s.at[n], fin_r.at[x], device(dest_x, iy, dest_zh, zi, cc))

    def stage_zh():
        for slot in range(3):
            zh_recv(slot).wait_recv()
        done[...] = zsum[zh] + zh_in[0] + zh_in[1] + zh_in[2]
        for n in range(4):
            pl.when(is_self[n])(lambda n=n: pltpu.make_async_copy(*fin_refs(n), fin_r.at[x]).start())
            pl.when(jnp.logical_not(is_self[n]))(lambda n=n: fin_copy(n).start())

    def stage_fin():
        for b in range(BLOCKS):
            remote(done.at[0:CUT, 0:256], fin_in.at[b], fin_s.at[0], fin_r.at[b], sibling).wait_recv()
            gram_ref[b] = fin_in[b] * (1.0 / 16384.0)

    mine = pl.ds(pl.multiple_of(zl * HALF, HALF), HALF)
    theirs = pl.ds(pl.multiple_of(other * HALF, HALF), HALF)

    def out_copy(o, t):
        to = device(mod(x + o, 4), y, zh, zl + t * (other - zl), c)
        return remote(bsend.at[o, t], bland.at[x, zl], out_s.at[o, t], out_r.at[x, zl], to)

    def out_recv(o, t):
        b, half = mod(x + o, 4), (zl, other)[t]
        return remote(bsend.at[o, t], bland.at[b, half], out_s.at[o, t], out_r.at[b, half], pooled(o, t))

    def basis(o):
        q = mod(x + o, 4)

        def rows_of(n, _):
            t = 1 - n
            prod = jnp.dot(ee[t].reshape(2 * PAD, KDIM), xs[q].reshape(KDIM, 2 * HALF), preferred_element_type=F32)
            bsend[o, t, 0] = (prod[:PAD, :HALF] - prod[PAD:, HALF:]).astype(jnp.bfloat16)
            bsend[o, t, 1] = (prod[PAD:, :HALF] + prod[:PAD, HALF:]).astype(jnp.bfloat16)
            own = (o == 0) & (t == 0)

            @pl.when(own)
            def _():
                basis_ref[0, x, :, mine] = bsend[0, 0, 0]
                basis_ref[1, x, :, mine] = bsend[0, 0, 1]

            pl.when(jnp.logical_not(own))(lambda: out_copy(o, t).start())
            return 0

        lax.fori_loop(0, 2, rows_of, 0)

    def basis_land(o, t):
        out_recv(o, t).wait_recv()
        b, half = mod(x + o, 4), (zl, other)[t]
        for part in range(2):
            basis_ref[part, b, :, (mine, theirs)[t]] = bland[b, half, part]

    for o in (0, 3, 1, 2):
        for t in (0, 1):
            if (o, t) != (0, 0):
                scat_recv(o, t).wait_recv()
                near(0, o, t).start()
                near(1, o, t).start()
    pack_eig()
    eig_copy().start()
    parts[...] = jnp.zeros(parts.shape, F32)

    def hop_one(i, _):
        o = jnp.where(i == 0, 0, jnp.where(i == 1, 3, i - 1))
        for way in (0, 1):
            near_recv(way, o, 0).wait_recv()
            near_recv(way, o, 1).wait_recv()
            ring(way, o, 2).start()
        gram_partial(0, o)
        return 0

    def hop_two(i, _):
        o = jnp.where(i == 0, 0, jnp.where(i == 1, 3, i - 1))
        for way in (0, 1):
            ring_recv(way, o, 2).wait_recv()
            ring(way, o, 3).start()
        gram_partial(1, o)
        pl.when(i == 0)(lambda: stage_core(0))
        return 0

    def hop_three(i, _):
        o = jnp.where(i == 0, 0, jnp.where(i == 1, 3, i - 1))
        for way in (0, 1):
            ring_recv(way, o, 3).wait_recv()
            ring(way, o, 4).start()

        @pl.when(i == 0)
        def _():
            stage_core(1)
            eig_copy().wait_recv()
            eig_forward().start()

        pl.when(i == 2)(lambda: stage_zl(1))
        return 0

    def hop_four(i, _):
        o = jnp.where(i == 0, 3, jnp.where(i == 3, 0, i))
        for way in (0, 1):
            ring_recv(way, o, 4).wait_recv()
        basis(o)
        pl.when(i == ZH_SLOT)(stage_zh)
        return 0

    lax.fori_loop(0, 4, hop_one, 0)
    core_copy(0).start()
    lax.fori_loop(0, 4, hop_two, 0)
    core_copy(1).start()
    pl.when(zh < 3)(lambda: pl.semaphore_wait(above, 3 - zh))
    stage_zl(0)
    lax.fori_loop(0, 4, hop_three, 0)
    eig_forward_recv().wait_recv()
    lax.fori_loop(0, 4, hop_four, 0)
    for o in (1, 3, 2):
        for t in (0, 1):
            basis_land(o, t)
    stage_fin()
    basis_land(0, 1)

    for o, t in pool:
        scat_copy(o, t).wait_send()
        out_copy(o, t).wait_send()
    for way in (0, 1):
        for o in range(4):
            near(way, o, 0).wait_send()
            near(way, o, 1).wait_send()
            for d in (2, 3, 4):
                ring(way, o, d).wait_send()
    eig_copy().wait_send()
    eig_forward().wait_send()
    for n in range(2):
        core_copy(n).wait_send()
        zl_copy(n).wait_send()
    for k in range(4):
        pl.when(zh != k)(lambda k=k: zh_copy(k).wait_send())
        pl.when(jnp.logical_not(is_self[k]))(lambda k=k: fin_copy(k).wait_send())


def local(responses, eigvecs):
    dma = pltpu.SemaphoreType.DMA
    bf, vm = jnp.bfloat16, pltpu.VMEM
    basis, gram = pl.pallas_call(
        kernel,
        out_shape=(
            jax.ShapeDtypeStruct((2, BLOCKS, PAD, 2 * HALF), bf),
            jax.ShapeDtypeStruct((BLOCKS, CUT, 256), F32),
        ),
        in_specs=[pl.BlockSpec(memory_space=vm), pl.BlockSpec(memory_space=pl.ANY)],
        out_specs=(pl.BlockSpec(memory_space=vm),) * 2,
        scratch_shapes=[
            vm((4, 2, RING, PAD, 2 * HALF), bf),
            vm((4, 2, PAD, 2 * HALF), bf),
            vm((2, ROWS, KDIM), bf),
            vm((2, 2, PAD, KDIM), bf),
            vm((4, 2, 2, PAD, HALF), bf),
            vm((4, 2, 2, PAD, HALF), bf),
            vm((2, 2, 2, 2 * PAD, 4 * PAD), F32),
            vm((2, 2, 2 * PAD, 4 * PAD), F32),
            vm((2, 2, PAD, 4 * PAD), F32),
            vm((4, PAD, 4 * PAD), F32),
            vm((3, PAD, 4 * PAD), F32),
            vm((PAD, 4 * PAD), F32),
            vm((BLOCKS, CUT, 256), F32),
            dma((4, 2)), dma((4, 2)), dma((2, 4, 2)), dma((2, 4, 2)), dma((2, 4, 3)), dma((2, 4, 3)),
            dma((2,)), dma, dma, dma, dma, dma((4, 2)), dma((4, 2)),
            dma((2,)), dma((2,)), dma((2,)), dma((2,)),
            dma((4,)), dma((3,)), dma((4,)), dma((4,)),
            pltpu.SemaphoreType.REGULAR,
        ],
        compiler_params=pltpu.CompilerParams(
            collective_id=0, has_side_effects=True, vmem_limit_bytes=60 * 2**20
        ),
    )(responses, eigvecs)
    zl = lax.axis_index("exc") // 8
    c = lax.axis_index("unk") % 2
    mine = lax.dynamic_slice(gram, (0, c * 5, zl * 64), (BLOCKS, 45, 2 * PAD))
    mine = mine.reshape(BLOCKS, 45, 2, PAD)[..., :ROWS]
    return jnp.transpose(mine, (2, 0, 3, 1)), basis[:, :, :ROWS]


def solution(mesh):
    specs = P(None, None, "exc", "unk")
    return jax.shard_map(local, mesh=mesh, in_specs=(specs, P("exc", None)), out_specs=(specs, specs), check_vma=False)
```

time: 509 us -> 102 us (0.20)
  the two profiles are of different devices: /device:TPU:1 before, /device:TPU:81 now
where the time goes in v2:
time: 102 us
  Pallas kernels  94.7 us (93%)
  local copies, waits for them, and re-layouts  6.67 us (7%)
    pallas_call x1, Pallas kernels, local(): pl.pallas_call(kernel, out_shape=(jax.ShapeDtypeStruct((2, BLOCKS, PAD, 2...  94.7 us
    unnamed x3, local copies, waits for them, and re-layouts  5.43 us

profile of v2, /device:TPU:81, one launch (start us, length us, event | category | flops | bytes accessed | tf_op | source)
XLA Modules:
  0.0 102.1 jit_solution(16502442724408143550)
XLA Ops:
  0.6 2.1 %copy.6.x_ref = bf16[2,4,90,512]{3,2,1,0:T(8,128)(2,1)} copy(bf16[2,4,90,512]{3,1,2,0:T(4,128)(2,1)} %param.2) | data formatting | bytes 1474560 | tf_op args[0]
  2.8 94.7 %shard_map.41 = (bf16[2,4,96,512]{3,2,1,0:T(8,128)(2,1)}, f32[4,56,256]{2,1,0:T(8,128)}) custom-call(bf16[2,4,90,512]{3,2,1,0:T(8,128)(2,1)} %copy.6.x_ref, bf16[90,11520]{1,0:T(8,128)(2,1)} %e_ref.1), custom_call_target="tpu_custom_call" | custom-call | tf_op jit(solution)/shard_map/pallas_call | solution.py:352
  97.5 1.1 %constant_dynamic-slice_fusion = f32[4,45,192]{2,1,0:T(8,128)S(1)} fusion(f32[4,56,256]{2,1,0:T(8,128)} %get-tuple-element.4, s32[]{:T(128)S(6)} %select_n.18, s32[]{:T(128)S(6)} %select_n.20), kind=kLoop, calls=%fused_computation.1 | loop fusion | bytes 276488 | tf_op jit(solution)/shard_map/dynamic_slice | solution.py:386
  98.6 0.2 reshape.8
  98.8 0.7 copy.8
  99.5 2.6 %copy.9 = bf16[2,4,90,512]{3,1,2,0:T(4,128)(2,1)} copy(bf16[2,4,90,512]{3,2,1,0:T(8,128)(2,1)} %bitcast.4) | data formatting | bytes 1474560
  (1 shorter events, 0.0 us)

commit v3 on v2

--- a/solution.py
+++ b/solution.py
@@ -10,8 +10,8 @@
 BLOCKS, RING, GROUPS = 4, 8, 16
 WAVES = ROWS * GROUPS
 KDIM = PAD * GROUPS
-ZH_SLOT = 1
-CUT = 56
+ZL_SLOT, ZH_SLOT = 1, 1
+HROWS, HPAD = 45, 48
 F32 = jnp.float32
 
 
@@ -45,16 +45,21 @@
     up, down = device(x, mod(y + 1, 8), zh, zl, c), device(x, mod(y - 1, 8), zh, zl, c)
     pair = device(x, y, zh, other, c)
     sibling = device(x, y, zh, zl, 1 - c)
-    pool = [(o, t) for o in (0, 1, 3, 2) for t in (0, 1) if (o, t) != (0, 0)]
+    pool = [(o, t) for o in (0, 1, 3, 2) for t in (1, 0) if (o, t) != (0, 0)]
 
     def pooled(o, t):
         return device(mod(x + o, 4), y, zh, (zl, other)[t], c)
 
-    jy, iy = mod(y + row_of(zh), 8), mod(y + col_of(zh, c), 8)
-    dests = [(zi, cc) for zi in (0, 1) for cc in (0, 1)]
-    dest_x, dest_zh = jy % 4, zl * 2 + jy // 4
-    same = (dest_x == x) & (iy == y) & (dest_zh == zh)
-    is_self = [same & (zl == zi) & (c == cc) for zi, cc in dests]
+    final_x, final_y, final_zh, is_self = [], [], [], []
+    for n in range(2):
+        k = 2 * n + zh // 2
+        jy, iy = mod(y + row_of(k), 8), mod(y + col_of(k, c), 8)
+        final_x.append(jy % 4)
+        final_y.append(iy)
+        final_zh.append(zl * 2 + jy // 4)
+        here = (final_x[n] == x) & (iy == y) & (final_zh[n] == zh) & (zh % 2 == c)
+        is_self.append([here & (zl == zi) for zi in (0, 1)])
+
     def remote(src, dst, send, recv, to):
         return pltpu.make_async_remote_copy(
             src_ref=src, dst_ref=dst, send_sem=send, recv_sem=recv, device_id=to, device_id_type=MESH
@@ -84,8 +89,6 @@
         def _():
             pl.semaphore_signal(above, inc=1, device_id=device(x, y, k, zl, c), device_id_type=MESH)
 
-    zero = jnp.zeros((PAD - 80, 2 * HALF), jnp.bfloat16)
-
     def scat_copy(o, t):
         return remote(staged.at[mod(x + o, 4), t], xs.at[x, zl, y], scat_s.at[o, t], scat_r.at[x, zl], pooled(o, t))
 
@@ -116,24 +119,21 @@
         ref = ring_ref(way, o, d, d)
         return remote(ref, ref, ring_s.at[way, o, d - 2], ring_r.at[way, o, d - 2], (up, down)[way])
 
-    for o in (0, 1, 3, 2):
-        b = mod(x + o, 4)
-        p, q = x_ref[0, b], x_ref[1, b]
-        low = jnp.concatenate([p[:, :HALF], q[:, :HALF]], axis=1)
-        high = jnp.concatenate([p[:, HALF:], q[:, HALF:]], axis=1)
-        first = jnp.full(low.shape, zl, jnp.int32) == 0
-        staged[b, 1, 80:96, :] = zero
-        staged[b, 1, 0:ROWS, :] = jnp.where(first, high, low)
-        scat_copy(o, 1).start()
-        if o == 0:
-            xs[b, zl, y, 80:96, :] = zero
-            xs[b, zl, y, 0:ROWS, :] = jnp.where(first, low, high)
-            near(0, 0, 0).start()
-            near(1, 0, 0).start()
-        else:
-            staged[b, 0, 80:96, :] = zero
-            staged[b, 0, 0:ROWS, :] = jnp.where(first, low, high)
-            scat_copy(o, 0).start()
+    staged[...] = jnp.zeros(staged.shape, jnp.bfloat16)
+    for b in range(BLOCKS):
+        for h in range(2):
+            p, q = [x_ref[part, h * HROWS : (h + 1) * HROWS, b, :] for part in range(2)]
+            low = jnp.concatenate([p[:, :HALF], q[:, :HALF]], axis=1)
+            high = jnp.concatenate([p[:, HALF:], q[:, HALF:]], axis=1)
+            first = jnp.full(low.shape, zl, jnp.int32) == 0
+            staged[b, 0, h * HPAD : h * HPAD + HROWS, :] = jnp.where(first, low, high)
+            staged[b, 1, h * HPAD : h * HPAD + HROWS, :] = jnp.where(first, high, low)
+    scat_copy(0, 1).start()
+    xs[x, zl, y] = staged[x, 0]
+    near(0, 0, 0).start()
+    near(1, 0, 0).start()
+    for o, t in pool[1:]:
+        scat_copy(o, t).start()
 
     def pack_eig():
         win_copy(0).wait()
@@ -145,9 +145,9 @@
             @pl.when(x == at)
             def _():
                 for part in range(2):
-                    for i in range(GROUPS):
-                        first = at * 32 + i * ROWS
-                        ee[0, part, 0:ROWS, i * PAD : i * PAD + ROWS] = window[part, :, first : first + ROWS]
+                    for i in range(2 * GROUPS):
+                        first = at * 32 + i * HROWS
+                        ee[0, part, 0:ROWS, i * HPAD : i * HPAD + HROWS] = window[part, :, first : first + HROWS]
 
     def eig_copy():
         return remote(ee.at[0, c], ee.at[1, c], eig_s, eig_r, pair)
@@ -169,63 +169,79 @@
                 v = xs[q, zi, mod(y + col_of(k, s), 8)]
                 cols += [v, jnp.concatenate([-v[:, HALF:], v[:, :HALF]], axis=1)]
             right = jnp.concatenate(cols, axis=0)
-            prod = lax.dot_general(rows, right, (((1,), (1,)), ((), ())), preferred_element_type=F32)
-            parts[n, s, t // 2] += prod
+            parts[k, s] += lax.dot_general(rows, right, (((1,), (1,)), ((), ())), preferred_element_type=F32)
             return 0
 
         lax.fori_loop(0, 4, one, 0)
 
-    def core_copy(n):
-        return remote(parts.at[n, 1 - c], core_in.at[n], core_s.at[n], core_r.at[n], sibling)
-
-    def zl_copy(n):
+    def core_copy(k):
+        return remote(parts.at[k, 1 - c], core_in.at[k], core_s.at[k], core_r.at[k], sibling)
+
+    def zl_copy(k):
         rows = pl.ds(pl.multiple_of(other * PAD, PAD), PAD)
-        return remote(parts.at[n, c, :, rows], zl_in.at[n], zl_s.at[n], zl_r.at[n], pair)
-
-    def zh_copy(k):
-        slot = mod(zh - k, 4) - 1
-        return remote(zsum.at[k], zh_in.at[slot], zh_s.at[k], zh_r.at[slot], device(x, y, k, zl, c))
-
-    def zh_recv(slot):
-        return remote(zsum.at[0], zh_in.at[slot], zh_s.at[0], zh_r.at[slot], sibling)
-
-    def stage_core(n):
-        core_copy(n).wait_recv()
-        for k in range(2):
-            parts[n, c, k] += core_in[n, k]
-        zl_copy(n).start()
-
-    def stage_zl(n):
-        zl_copy(n).wait_recv()
-        rows = pl.ds(pl.multiple_of(zl * PAD, PAD), PAD)
-        for k in range(2):
-            zsum[2 * n + k] = parts[n, c, k, rows] + zl_in[n, k]
-            pl.when(zh != 2 * n + k)(lambda k=k: zh_copy(2 * n + k).start())
-
-    def fin_refs(n):
-        zi, cc = dests[n]
-        return done.at[40 * cc : 40 * cc + CUT, zi * 128 : zi * 128 + 256], fin_in.at[x]
-
-    def fin_copy(n):
-        zi, cc = dests[n]
-        src, dst = fin_refs(n)
-        return remote(src, dst, fin_s.at[n], fin_r.at[x], device(dest_x, iy, dest_zh, zi, cc))
-
-    def stage_zh():
+        return remote(parts.at[k, c, rows], zl_in.at[k], zl_s.at[k], zl_r.at[k], pair)
+
+    def zh_copy(k, h):
+        to = (k % 2) * 2 + h
+        slot = mod(zh - to, 4) - 1
+        return remote(
+            zsum.at[k, h * HPAD : (h + 1) * HPAD], zh_in.at[k // 2, slot],
+            zh_s.at[k, h], zh_r.at[k // 2, slot], device(x, y, to, zl, c),
+        )
+
+    def zh_recv(n, slot):
+        return remote(zsum.at[0, 0:HPAD], zh_in.at[n, slot], zh_s.at[0, 0], zh_r.at[n, slot], sibling)
+
+    def stage_core(k):
+        core_copy(k).wait_recv()
+        parts[k, c] += core_in[k]
+        zl_copy(k).start()
+
+    def stage_zl(k):
+        zl_copy(k).wait_recv()
+        zsum[k] = parts[k, c, pl.ds(pl.multiple_of(zl * PAD, PAD), PAD)] + zl_in[k]
+        for h in (0, 1):
+            pl.when(zh != (k % 2) * 2 + h)(lambda h=h: zh_copy(k, h).start())
+
+    def fin_refs(n, zi):
+        return done.at[n, :, zi * 128 : zi * 128 + 256], fin_in.at[x]
+
+    def fin_copy(n, zi):
+        src, dst = fin_refs(n, zi)
+        to = device(final_x[n], final_y[n], final_zh[n], zi, zh % 2)
+        return remote(src, dst, fin_s.at[n, zi], fin_r.at[x], to)
+
+    def stage_zh(n):
         for slot in range(3):
-            zh_recv(slot).wait_recv()
-        done[...] = zsum[zh] + zh_in[0] + zh_in[1] + zh_in[2]
-        for n in range(4):
-            pl.when(is_self[n])(lambda n=n: pltpu.make_async_copy(*fin_refs(n), fin_r.at[x]).start())
-            pl.when(jnp.logical_not(is_self[n]))(lambda n=n: fin_copy(n).start())
+            zh_recv(n, slot).wait_recv()
+        rows = pl.ds(pl.multiple_of((zh % 2) * HPAD, HPAD), HPAD)
+        done[n] = zsum[2 * n + zh // 2, rows] + zh_in[n, 0] + zh_in[n, 1] + zh_in[n, 2]
+        for zi in (0, 1):
+            pl.when(is_self[n][zi])(lambda zi=zi: pltpu.make_async_copy(*fin_refs(n, zi), fin_r.at[x]).start())
+            pl.when(jnp.logical_not(is_self[n][zi]))(lambda zi=zi: fin_copy(n, zi).start())
 
     def stage_fin():
+        left = jnp.full((HROWS, HROWS), zl, jnp.int32) == 0
         for b in range(BLOCKS):
-            remote(done.at[0:CUT, 0:256], fin_in.at[b], fin_s.at[0], fin_r.at[b], sibling).wait_recv()
-            gram_ref[b] = fin_in[b] * (1.0 / 16384.0)
+            remote(done.at[0, :, 0:256], fin_in.at[b], fin_s.at[0, 0], fin_r.at[b], sibling).wait_recv()
+            v = fin_in[b, 0:HROWS] * (1.0 / 16384.0)
+            for part in range(2):
+                for h in range(2):
+                    at = part * PAD + h * HPAD
+                    gram_ref[part, :, b, h * HROWS : (h + 1) * HROWS] = jnp.where(
+                        left, v[:, at : at + HROWS], v[:, 64 + at : 64 + at + HROWS]
+                    )
 
     mine = pl.ds(pl.multiple_of(zl * HALF, HALF), HALF)
     theirs = pl.ds(pl.multiple_of(other * HALF, HALF), HALF)
+
+    def put(b, lanes, rows):
+        for at in range(BLOCKS):
+
+            @pl.when(b == at)
+            def _():
+                for part in range(2):
+                    basis_ref[part, :, at, lanes] = rows[part, 0:ROWS]
 
     def out_copy(o, t):
         to = device(mod(x + o, 4), y, zh, zl + t * (other - zl), c)
@@ -247,8 +263,7 @@
 
             @pl.when(own)
             def _():
-                basis_ref[0, x, :, mine] = bsend[0, 0, 0]
-                basis_ref[1, x, :, mine] = bsend[0, 0, 1]
+                put(x, mine, bsend.at[0, 0])
 
             pl.when(jnp.logical_not(own))(lambda: out_copy(o, t).start())
             return 0
@@ -258,8 +273,7 @@
     def basis_land(o, t):
         out_recv(o, t).wait_recv()
         b, half = mod(x + o, 4), (zl, other)[t]
-        for part in range(2):
-            basis_ref[part, b, :, (mine, theirs)[t]] = bland[b, half, part]
+        put(b, (mine, theirs)[t], bland.at[b, half])
 
     for o in (0, 3, 1, 2):
         for t in (0, 1):
@@ -286,7 +300,13 @@
             ring_recv(way, o, 2).wait_recv()
             ring(way, o, 3).start()
         gram_partial(1, o)
-        pl.when(i == 0)(lambda: stage_core(0))
+
+        @pl.when(i == 2)
+        def _():
+            pl.when(zh < 3)(lambda: pl.semaphore_wait(above, 3 - zh))
+            stage_zl(0)
+            stage_zl(1)
+
         return 0
 
     def hop_three(i, _):
@@ -297,11 +317,16 @@
 
         @pl.when(i == 0)
         def _():
-            stage_core(1)
             eig_copy().wait_recv()
             eig_forward().start()
 
-        pl.when(i == 2)(lambda: stage_zl(1))
+        pl.when(i == ZL_SLOT)(lambda: stage_zl(2))
+
+        @pl.when(i == ZL_SLOT + 1)
+        def _():
+            stage_zl(3)
+            stage_zh(0)
+
         return 0
 
     def hop_four(i, _):
@@ -309,15 +334,19 @@
         for way in (0, 1):
             ring_recv(way, o, 4).wait_recv()
         basis(o)
-        pl.when(i == ZH_SLOT)(stage_zh)
+        pl.when(i == ZH_SLOT + zh // 2)(lambda: stage_zh(1))
         return 0
 
     lax.fori_loop(0, 4, hop_one, 0)
-    core_copy(0).start()
+    for k in (0, 1):
+        core_copy(k).start()
+    for k in (0, 1):
+        stage_core(k)
     lax.fori_loop(0, 4, hop_two, 0)
-    core_copy(1).start()
-    pl.when(zh < 3)(lambda: pl.semaphore_wait(above, 3 - zh))
-    stage_zl(0)
+    for k in (2, 3):
+        core_copy(k).start()
+    for k in (2, 3):
+        stage_core(k)
     lax.fori_loop(0, 4, hop_three, 0)
     eig_forward_recv().wait_recv()
     lax.fori_loop(0, 4, hop_four, 0)
@@ -338,12 +367,25 @@
                 ring(way, o, d).wait_send()
     eig_copy().wait_send()
     eig_forward().wait_send()
+    for k in range(4):
+        core_copy(k).wait_send()
+        zl_copy(k).wait_send()
+        for h in (0, 1):
+            pl.when(zh != (k % 2) * 2 + h)(lambda k=k, h=h: zh_copy(k, h).wait_send())
     for n in range(2):
-        core_copy(n).wait_send()
-        zl_copy(n).wait_send()
-    for k in range(4):
-        pl.when(zh != k)(lambda k=k: zh_copy(k).wait_send())
-        pl.when(jnp.logical_not(is_self[k]))(lambda k=k: fin_copy(k).wait_send())
+        for zi in (0, 1):
+            pl.when(jnp.logical_not(is_self[n][zi]))(lambda n=n, zi=zi: fin_copy(n, zi).wait_send())
+
+
+def hand_on(basis_ref, gram_ref, basis_out, gram_out, basis_sem, gram_sem):
+    copies = []
+    for part in range(2):
+        copies.append(pltpu.make_async_copy(basis_ref.at[part], basis_out.at[part], basis_sem.at[part]))
+        copies.append(pltpu.make_async_copy(gram_ref.at[part], gram_out.at[part], gram_sem.at[part]))
+    for copy in copies:
+        copy.start()
+    for copy in copies:
+        copy.wait()
 
 
 def local(responses, eigvecs):
@@ -352,8 +394,8 @@
     basis, gram = pl.pallas_call(
         kernel,
         out_shape=(
-            jax.ShapeDtypeStruct((2, BLOCKS, PAD, 2 * HALF), bf),
-            jax.ShapeDtypeStruct((BLOCKS, CUT, 256), F32),
+            jax.ShapeDtypeStruct((2, ROWS, BLOCKS, 2 * HALF), bf),
+            jax.ShapeDtypeStruct((2, 45, BLOCKS, ROWS), F32),
         ),
         in_specs=[pl.BlockSpec(memory_space=vm), pl.BlockSpec(memory_space=pl.ANY)],
         out_specs=(pl.BlockSpec(memory_space=vm),) * 2,
@@ -364,28 +406,31 @@
             vm((2, 2, PAD, KDIM), bf),
             vm((4, 2, 2, PAD, HALF), bf),
             vm((4, 2, 2, PAD, HALF), bf),
-            vm((2, 2, 2, 2 * PAD, 4 * PAD), F32),
-            vm((2, 2, 2 * PAD, 4 * PAD), F32),
-            vm((2, 2, PAD, 4 * PAD), F32),
+            vm((4, 2, 2 * PAD, 4 * PAD), F32),
+            vm((4, 2 * PAD, 4 * PAD), F32),
             vm((4, PAD, 4 * PAD), F32),
-            vm((3, PAD, 4 * PAD), F32),
-            vm((PAD, 4 * PAD), F32),
-            vm((BLOCKS, CUT, 256), F32),
+            vm((4, PAD, 4 * PAD), F32),
+            vm((2, 3, HPAD, 4 * PAD), F32),
+            vm((2, HPAD, 4 * PAD), F32),
+            vm((BLOCKS, HPAD, 256), F32),
             dma((4, 2)), dma((4, 2)), dma((2, 4, 2)), dma((2, 4, 2)), dma((2, 4, 3)), dma((2, 4, 3)),
             dma((2,)), dma, dma, dma, dma, dma((4, 2)), dma((4, 2)),
-            dma((2,)), dma((2,)), dma((2,)), dma((2,)),
-            dma((4,)), dma((3,)), dma((4,)), dma((4,)),
+            dma((4,)), dma((4,)), dma((4,)), dma((4,)),
+            dma((4, 2)), dma((2, 3)), dma((2, 2)), dma((4,)),
             pltpu.SemaphoreType.REGULAR,
         ],
         compiler_params=pltpu.CompilerParams(
             collective_id=0, has_side_effects=True, vmem_limit_bytes=60 * 2**20
         ),
-    )(responses, eigvecs)
-    zl = lax.axis_index("exc") // 8
-    c = lax.axis_index("unk") % 2
-    mine = lax.dynamic_slice(gram, (0, c * 5, zl * 64), (BLOCKS, 45, 2 * PAD))
-    mine = mine.reshape(BLOCKS, 45, 2, PAD)[..., :ROWS]
-    return jnp.transpose(mine, (2, 0, 3, 1)), basis[:, :, :ROWS]
+    )(jnp.transpose(responses, (0, 2, 1, 3)), eigvecs)
+    basis, gram = pl.pallas_call(
+        hand_on,
+        out_shape=(jax.ShapeDtypeStruct(basis.shape, bf), jax.ShapeDtypeStruct(gram.shape, F32)),
+        in_specs=[pl.BlockSpec(memory_space=vm)] * 2,
+        out_specs=(pl.BlockSpec(memory_space=pl.ANY),) * 2,
+        scratch_shapes=[dma((2,)), dma((2,))],
+    )(basis, gram)
+    return jnp.transpose(gram, (0, 2, 3, 1)), jnp.transpose(basis, (0, 2, 1, 3))
 
 
 def solution(mesh):

time: 102 us -> 91.1 us (0.89)
  the two profiles are of different devices: /device:TPU:81 before, /device:TPU:1 now
where the time goes in v3:
time: 91.1 us; the launch traced here: 90.1 us
  Pallas kernels  89.4 us (98%)
    pallas_call x1, Pallas kernels, local(): pl.pallas_call(kernel, out_shape=(jax.ShapeDtypeStruct((2, ROWS, BLOCKS,...  87.3 us
    pallas_call x1, Pallas kernels, local(): pl.pallas_call(hand_on, out_shape=(jax.ShapeDtypeStruct(basis.shape, bf),...  2.09 us

profile of v3, /device:TPU:1, one launch (start us, length us, event | category | flops | bytes accessed | tf_op | source)
XLA Modules:
  0.0 90.1 jit_solution(14849331648010632657)
XLA Ops:
  0.6 87.3 %shard_map.41 = (bf16[2,90,4,512]{3,2,1,0:T(4,128)(2,1)}, f32[2,45,4,90]{3,2,1,0:T(4,128)}) custom-call(bf16[2,90,4,512]{3,2,1,0:T(4,128)(2,1)} %bitcast.3, bf16[90,11520]{1,0:T(8,128)(2,1)} %e_ref.1), custom_call_target="tpu_custom_call" | custom-call | tf_op jit(solution)/shard_map/pallas_call | solution.py:394
  88.0 2.1 %shard_map.42 = (bf16[2,90,4,512]{3,2,1,0:T(4,128)(2,1)}, f32[2,45,4,90]{3,2,1,0:T(4,128)}) custom-call(bf16[2,90,4,512]{3,2,1,0:T(4,128)(2,1)} %get-tuple-element.6.basis_ref, f32[2,45,4,90]{3,2,1,0:T(4,128)} %get-tuple-element.7.gram_ref), custom_call_target="tpu_custom_call" | custom-call | tf_op jit(solution)/shard_map/pallas_call | solution.py:426

commit v4 on v3

--- a/solution.py
+++ b/solution.py
@@ -33,9 +33,9 @@
 
 
 def kernel(
-    x_ref, e_ref, basis_ref, gram_ref,
-    xs, staged, window, ee, bsend, bland, parts, core_in, zl_in, zsum, zh_in, done, fin_in,
-    scat_s, scat_r, near_s, near_r, ring_s, ring_r, win_s, eig_s, eig_r, fwd_s, fwd_r, out_s, out_r,
+    x_hbm, e_ref, basis_ref, gram_ref,
+    x_ref, xs, staged, window, ee, bsend, bland, parts, core_in, zl_in, zsum, zh_in, done, fin_in,
+    x_sem, scat_s, scat_r, near_s, near_r, ring_s, ring_r, win_s, eig_s, eig_r, fwd_s, fwd_r, out_s, out_r,
     core_s, core_r, zl_s, zl_r, zh_s, zh_r, fin_s, fin_r, above,
 ):
     exc, unk = lax.axis_index("exc"), lax.axis_index("unk")
@@ -69,6 +69,9 @@
         first = pl.multiple_of((part * 4 + x) * 1408 + part * 128, 128)
         return pltpu.make_async_copy(e_ref.at[:, pl.ds(first, KDIM)], window.at[part], win_s.at[part])
 
+    x_copies = [pltpu.make_async_copy(x_hbm.at[part], x_ref.at[part], x_sem.at[part]) for part in range(2)]
+    for copy in x_copies:
+        copy.start()
     win_copy(0).start()
     win_copy(1).start()
 
@@ -82,12 +85,6 @@
         greet(to)
     for k in (1, 2, 3):
         pl.when(zh < k)(lambda k=k: greet(device(x, y, k, zl, c)))
-    pl.semaphore_wait(barrier, len(around) + zh)
-    for k in (0, 1, 2):
-
-        @pl.when(zh > k)
-        def _():
-            pl.semaphore_signal(above, inc=1, device_id=device(x, y, k, zl, c), device_id_type=MESH)
 
     def scat_copy(o, t):
         return remote(staged.at[mod(x + o, 4), t], xs.at[x, zl, y], scat_s.at[o, t], scat_r.at[x, zl], pooled(o, t))
@@ -120,6 +117,8 @@
         return remote(ref, ref, ring_s.at[way, o, d - 2], ring_r.at[way, o, d - 2], (up, down)[way])
 
     staged[...] = jnp.zeros(staged.shape, jnp.bfloat16)
+    for copy in x_copies:
+        copy.wait()
     for b in range(BLOCKS):
         for h in range(2):
             p, q = [x_ref[part, h * HROWS : (h + 1) * HROWS, b, :] for part in range(2)]
@@ -128,8 +127,16 @@
             first = jnp.full(low.shape, zl, jnp.int32) == 0
             staged[b, 0, h * HPAD : h * HPAD + HROWS, :] = jnp.where(first, low, high)
             staged[b, 1, h * HPAD : h * HPAD + HROWS, :] = jnp.where(first, high, low)
+    xs[x, zl, y] = staged[x, 0]
+
+    pl.semaphore_wait(barrier, len(around) + zh)
+    for k in (0, 1, 2):
+
+        @pl.when(zh > k)
+        def _():
+            pl.semaphore_signal(above, inc=1, device_id=device(x, y, k, zl, c), device_id_type=MESH)
+
     scat_copy(0, 1).start()
-    xs[x, zl, y] = staged[x, 0]
     near(0, 0, 0).start()
     near(1, 0, 0).start()
     for o, t in pool[1:]:
@@ -313,7 +320,7 @@
         o = jnp.where(i == 0, 0, jnp.where(i == 1, 3, i - 1))
         for way in (0, 1):
             ring_recv(way, o, 3).wait_recv()
-            ring(way, o, 4).start()
+            pl.when(i >= 2)(lambda way=way: ring(way, 3 - 2 * (i - 2), 4).start())
 
         @pl.when(i == 0)
         def _():
@@ -333,8 +340,9 @@
         o = jnp.where(i == 0, 3, jnp.where(i == 3, 0, i))
         for way in (0, 1):
             ring_recv(way, o, 4).wait_recv()
+            pl.when(i < 2)(lambda way=way: ring(way, 2 - 2 * i, 4).start())
         basis(o)
-        pl.when(i == ZH_SLOT + zh // 2)(lambda: stage_zh(1))
+        pl.when(i == ZH_SLOT)(lambda: stage_zh(1))
         return 0
 
     lax.fori_loop(0, 4, hop_one, 0)
@@ -397,9 +405,10 @@
             jax.ShapeDtypeStruct((2, ROWS, BLOCKS, 2 * HALF), bf),
             jax.ShapeDtypeStruct((2, 45, BLOCKS, ROWS), F32),
         ),
-        in_specs=[pl.BlockSpec(memory_space=vm), pl.BlockSpec(memory_space=pl.ANY)],
+        in_specs=[pl.BlockSpec(memory_space=pl.ANY)] * 2,
         out_specs=(pl.BlockSpec(memory_space=vm),) * 2,
         scratch_shapes=[
+            vm((2, ROWS, BLOCKS, 2 * HALF), bf),
             vm((4, 2, RING, PAD, 2 * HALF), bf),
             vm((4, 2, PAD, 2 * HALF), bf),
             vm((2, ROWS, KDIM), bf),
@@ -413,7 +422,7 @@
             vm((2, 3, HPAD, 4 * PAD), F32),
             vm((2, HPAD, 4 * PAD), F32),
             vm((BLOCKS, HPAD, 256), F32),
-            dma((4, 2)), dma((4, 2)), dma((2, 4, 2)), dma((2, 4, 2)), dma((2, 4, 3)), dma((2, 4, 3)),
+            dma((2,)), dma((4, 2)), dma((4, 2)), dma((2, 4, 2)), dma((2, 4, 2)), dma((2, 4, 3)), dma((2, 4, 3)),
             dma((2,)), dma, dma, dma, dma, dma((4, 2)), dma((4, 2)),
             dma((4,)), dma((4,)), dma((4,)), dma((4,)),
             dma((4, 2)), dma((2, 3)), dma((2, 2)), dma((4,)),

time: 91.1 us -> 88.3 us (0.969)
  Pallas kernels: 89.4 us -> 87 us
    pallas_call x1, Pallas kernels: 87.3 us -> 85 us  [local(): pl.pallas_call(kernel, out_shape=(jax.ShapeDtypeStruct((2, ROWS, BLOCKS,...]
where the time goes in v4:
time: 88.3 us; the launch traced here: 87.7 us
  Pallas kernels  87 us (99%)
    pallas_call x1, Pallas kernels, local(): pl.pallas_call(kernel, out_shape=(jax.ShapeDtypeStruct((2, ROWS, BLOCKS,...  85 us
    pallas_call x1, Pallas kernels, local(): pl.pallas_call(hand_on, out_shape=(jax.ShapeDtypeStruct(basis.shape, bf),...  2.09 us

profile of v4, /device:TPU:1, one launch (start us, length us, event | category | flops | bytes accessed | tf_op | source)
XLA Modules:
  0.0 87.7 jit_solution(14261982436995503636)
XLA Ops:
  0.6 85.0 %shard_map.41 = (bf16[2,90,4,512]{3,2,1,0:T(4,128)(2,1)}, f32[2,45,4,90]{3,2,1,0:T(4,128)}) custom-call(bf16[2,90,4,512]{3,2,1,0:T(4,128)(2,1)} %bitcast.3, bf16[90,11520]{1,0:T(8,128)(2,1)} %e_ref.1), custom_call_target="tpu_custom_call" | custom-call | tf_op jit(solution)/shard_map/pallas_call | solution.py:402
  85.6 2.1 %shard_map.42 = (bf16[2,90,4,512]{3,2,1,0:T(4,128)(2,1)}, f32[2,45,4,90]{3,2,1,0:T(4,128)}) custom-call(bf16[2,90,4,512]{3,2,1,0:T(4,128)(2,1)} %get-tuple-element.6.basis_ref, f32[2,45,4,90]{3,2,1,0:T(4,128)} %get-tuple-element.7.gram_ref), custom_call_target="tpu_custom_call" | custom-call | tf_op jit(solution)/shard_map/pallas_call | solution.py:435

commit v5 on v4

--- a/solution.py
+++ b/solution.py
@@ -10,7 +10,7 @@
 BLOCKS, RING, GROUPS = 4, 8, 16
 WAVES = ROWS * GROUPS
 KDIM = PAD * GROUPS
-ZL_SLOT, ZH_SLOT = 1, 1
+ZL_SLOT, ZH_SLOT = 0, 1
 HROWS, HPAD = 45, 48
 F32 = jnp.float32
 
@@ -169,7 +169,7 @@
         q = mod(x + o, 4)
 
         def one(t, _):
-            k, s = 2 * n + t // 2, t % 2
+            k, s = (t // 2 + t // 4, t % 2) if n == 0 else (2 + t // 2, t % 2 + t // 2)
             rows = xs[q, :, mod(y + row_of(k), 8)].reshape(2 * PAD, 2 * HALF)
             cols = []
             for zi in range(2):
@@ -179,7 +179,7 @@
             parts[k, s] += lax.dot_general(rows, right, (((1,), (1,)), ((), ())), preferred_element_type=F32)
             return 0
 
-        lax.fori_loop(0, 4, one, 0)
+        lax.fori_loop(0, 5 - 2 * n, one, 0)
 
     def core_copy(k):
         return remote(parts.at[k, 1 - c], core_in.at[k], core_s.at[k], core_r.at[k], sibling)
@@ -313,6 +313,7 @@
             pl.when(zh < 3)(lambda: pl.semaphore_wait(above, 3 - zh))
             stage_zl(0)
             stage_zl(1)
+            pl.when(c == 0)(lambda: stage_zl(3))
 
         return 0
 
@@ -328,11 +329,11 @@
             eig_forward().start()
 
         pl.when(i == ZL_SLOT)(lambda: stage_zl(2))
+        pl.when(i == 3)(lambda: stage_zh(0))
 
         @pl.when(i == ZL_SLOT + 1)
         def _():
-            stage_zl(3)
-            stage_zh(0)
+            pl.when(c == 1)(lambda: stage_zl(3))
 
         return 0
 
@@ -348,13 +349,15 @@
     lax.fori_loop(0, 4, hop_one, 0)
     for k in (0, 1):
         core_copy(k).start()
+    pl.when(c == 1)(lambda: core_copy(3).start())
     for k in (0, 1):
         stage_core(k)
+    pl.when(c == 0)(lambda: stage_core(3))
     lax.fori_loop(0, 4, hop_two, 0)
-    for k in (2, 3):
-        core_copy(k).start()
-    for k in (2, 3):
-        stage_core(k)
+    core_copy(2).start()
+    pl.when(c == 0)(lambda: core_copy(3).start())
+    stage_core(2)
+    pl.when(c == 1)(lambda: stage_core(3))
     lax.fori_loop(0, 4, hop_three, 0)
     eig_forward_recv().wait_recv()
     lax.fori_loop(0, 4, hop_four, 0)

time: 88.3 us -> 88 us (level)
  no operation moved by 1% of the time
where the time goes in v5:
time: 88 us; the launch traced here: 87.1 us
  Pallas kernels  86.5 us (98%)
    pallas_call x1, Pallas kernels, local(): pl.pallas_call(kernel, out_shape=(jax.ShapeDtypeStruct((2, ROWS, BLOCKS,...  84.4 us
    pallas_call x1, Pallas kernels, local(): pl.pallas_call(hand_on, out_shape=(jax.ShapeDtypeStruct(basis.shape, bf),...  2.09 us

profile of v5, /device:TPU:1, one launch (start us, length us, event | category | flops | bytes accessed | tf_op | source)
XLA Modules:
  0.0 87.1 jit_solution(3975430251373350556)
XLA Ops:
  0.6 84.4 %shard_map.41 = (bf16[2,90,4,512]{3,2,1,0:T(4,128)(2,1)}, f32[2,45,4,90]{3,2,1,0:T(4,128)}) custom-call(bf16[2,90,4,512]{3,2,1,0:T(4,128)(2,1)} %bitcast.3, bf16[90,11520]{1,0:T(8,128)(2,1)} %e_ref.1), custom_call_target="tpu_custom_call" | custom-call | tf_op jit(solution)/shard_map/pallas_call | solution.py:405
  85.0 2.1 %shard_map.42 = (bf16[2,90,4,512]{3,2,1,0:T(4,128)(2,1)}, f32[2,45,4,90]{3,2,1,0:T(4,128)}) custom-call(bf16[2,90,4,512]{3,2,1,0:T(4,128)(2,1)} %get-tuple-element.6.basis_ref, f32[2,45,4,90]{3,2,1,0:T(4,128)} %get-tuple-element.7.gram_ref), custom_call_target="tpu_custom_call" | custom-call | tf_op jit(solution)/shard_map/pallas_call | solution.py:438

commit v6 on v5

--- a/solution.py
+++ b/solution.py
@@ -321,7 +321,7 @@
         o = jnp.where(i == 0, 0, jnp.where(i == 1, 3, i - 1))
         for way in (0, 1):
             ring_recv(way, o, 3).wait_recv()
-            pl.when(i >= 2)(lambda way=way: ring(way, 3 - 2 * (i - 2), 4).start())
+            ring(way, o, 4).start()
 
         @pl.when(i == 0)
         def _():
@@ -341,7 +341,6 @@
         o = jnp.where(i == 0, 3, jnp.where(i == 3, 0, i))
         for way in (0, 1):
             ring_recv(way, o, 4).wait_recv()
-            pl.when(i < 2)(lambda way=way: ring(way, 2 - 2 * i, 4).start())
         basis(o)
         pl.when(i == ZH_SLOT)(lambda: stage_zh(1))
         return 0

time: 88 us -> 88.8 us (level)
  no operation moved by 1% of the time
where the time goes in v6:
time: 88.8 us; the launch traced here: 87.7 us
  Pallas kernels  87.1 us (98%)
    pallas_call x1, Pallas kernels, local(): pl.pallas_call(kernel, out_shape=(jax.ShapeDtypeStruct((2, ROWS, BLOCKS,...  85 us
    pallas_call x1, Pallas kernels, local(): pl.pallas_call(hand_on, out_shape=(jax.ShapeDtypeStruct(basis.shape, bf),...  2.09 us

profile of v6, /device:TPU:1, one launch (start us, length us, event | category | flops | bytes accessed | tf_op | source)
XLA Modules:
  0.0 87.7 jit_solution(4082289414854602199)
XLA Ops:
  0.6 85.0 %shard_map.41 = (bf16[2,90,4,512]{3,2,1,0:T(4,128)(2,1)}, f32[2,45,4,90]{3,2,1,0:T(4,128)}) custom-call(bf16[2,90,4,512]{3,2,1,0:T(4,128)(2,1)} %bitcast.3, bf16[90,11520]{1,0:T(8,128)(2,1)} %e_ref.1), custom_call_target="tpu_custom_call" | custom-call | tf_op jit(solution)/shard_map/pallas_call | solution.py:404
  85.6 2.1 %shard_map.42 = (bf16[2,90,4,512]{3,2,1,0:T(4,128)(2,1)}, f32[2,45,4,90]{3,2,1,0:T(4,128)}) custom-call(bf16[2,90,4,512]{3,2,1,0:T(4,128)(2,1)} %get-tuple-element.6.basis_ref, f32[2,45,4,90]{3,2,1,0:T(4,128)} %get-tuple-element.7.gram_ref), custom_call_target="tpu_custom_call" | custom-call | tf_op jit(solution)/shard_map/pallas_call | solution.py:437
